TPU v7x, 32 devices: a whole 2x2x4 slice. The times are simulated.
32 devices in a mesh: groups: 2 (over x), kv: 16 (over z, y, core).
Axes of the slice: x: 2, y: 2, z: 4, core: 2. Of those that a mesh axis runs over, the one named last changes fastest.
Arguments:
- query_in: bfloat16 [256, 2048], P(('groups', 'kv')), parts along dimension 0, may hold values from -6 to 6
- key_in: bfloat16 [256, 512], P(('groups', 'kv')), parts along dimension 0, may hold values from -16 to 16
- value_in: bfloat16 [256, 512], P(('groups', 'kv')), parts along dimension 0, may hold values from -6 to 6
- cache_keys: bfloat16 [4, 6144, 512], P('groups', 'kv'), parts along dimension 0, may hold values from -700 to 700
- cache_values: bfloat16 [4, 6144, 512], P('groups', 'kv'), parts along dimension 0, may hold values from -6 to 6
- live_slots: int32 [4, 16], P('groups', 'kv'), parts along dimension 0, may hold values from 0 to 384, as said below
- span_starts: int32 [4], P('groups'), parts along dimension 0, may hold values from 0 to 1048447
Outputs:
- attended: bfloat16 [256, 2048], P(('groups', 'kv')), parts along dimension 0
There are 2 independent parts, one for each index of `groups`. A program takes and returns all parts, laid end to end along the dimension named above; each array names one. Nothing has to cross between parts.
Inputs may be any that keep to these rules, and one draw needn't show every extreme that they name: `live_slots`: in every block some device has all 384 of its slots live.
All inputs are finite; a program needn't handle non-finite values.
Results may differ from a plain program's by a relative error of at most 0.006.
The roundings to bfloat16 on the way count: a program that leaves them out, or rounds other values in their place, can miss the bound.
Values may be sent and summed in bfloat16 or wider, within the bound.
A program may use at most 320 MiB of HBM per device.

v0:
```python
import jax
import jax.numpy as jnp
import numpy as np
from jax import lax
from jax.sharding import PartitionSpec as P

HD = 128


NEG_FILL = -1e30


def turn_table(head_size):
    half_size = head_size // 2
    frequency = 500000.0 ** (-np.arange(half_size) * 2.0 / head_size)
    turn_counts = np.floor(frequency / (2.0 * np.pi) * 2.0**32 + 0.5).astype(np.int64) % 2**32
    turn_counts = np.where(turn_counts >= 2**31, turn_counts - 2**32, turn_counts)
    return jnp.asarray(turn_counts.astype(np.int32))


def rotate_pairs(values, positions):
    half_size = values.shape[-1] // 2
    phases = positions[:, None] * turn_table(values.shape[-1])[None, :]
    angles = phases.astype(jnp.float32) * (2.0 * np.pi / 2.0**32)
    cosine = jnp.cos(angles)[:, None, :]
    sine_table = jnp.sin(angles)[:, None, :]
    first_half = values[..., :half_size]
    second_half = values[..., half_size:]
    return jnp.concatenate(
        [
            first_half * cosine - second_half * sine_table,
            second_half * cosine + first_half * sine_table,
        ],
        axis=-1,
    )


def partial_block(query_rows, block_keys, block_values, allowed):
    row_count = query_rows.shape[0]
    kv_heads = block_keys.shape[1]
    head_size = block_keys.shape[2]
    grouped = query_rows.reshape(row_count, kv_heads, -1, head_size)
    scores = jnp.einsum(
        "rkgd,skd->kgrs", grouped, block_keys, preferred_element_type=jnp.float32
    ) * head_size ** (-0.5)
    scores = jnp.where(allowed, scores, NEG_FILL)
    maxima = jnp.max(scores, axis=-1)
    weights = jnp.where(allowed, jnp.exp(scores - maxima[..., None]), 0.0)
    totals = jnp.sum(weights, axis=-1)
    weighted_sum = jnp.einsum(
        "kgrs,skd->rkgd",
        weights.astype(jnp.bfloat16),
        block_values,
        preferred_element_type=jnp.float32,
    )
    return (
        jnp.transpose(maxima, (2, 0, 1)).reshape(row_count, -1),
        jnp.transpose(totals, (2, 0, 1)).reshape(row_count, -1),
        weighted_sum.reshape(row_count, -1),
    )


def fold_pair(first_terms, second_terms):
    first_max, first_total, first_sum = first_terms
    second_max, second_total, second_sum = second_terms
    joint_max = jnp.maximum(first_max, second_max)
    first_factor = jnp.exp(first_max - joint_max)
    second_factor = jnp.exp(second_max - joint_max)
    row_count, head_count = joint_max.shape
    weighted = (
        first_sum.reshape(row_count, head_count, -1) * first_factor[..., None]
        + second_sum.reshape(row_count, head_count, -1) * second_factor[..., None]
    )
    return (
        joint_max,
        first_total * first_factor + second_total * second_factor,
        weighted.reshape(row_count, -1),
    )


def rescale(local_max, local_total, local_sum, global_max):
    factor = jnp.exp(local_max - global_max)
    row_count, head_count = factor.shape
    scaled_sum = (local_sum.reshape(row_count, head_count, -1) * factor[..., None]).reshape(
        row_count, -1
    )
    return (local_total * factor, scaled_sum)


def normalize(combined):
    unused_max, totals, sums = combined
    row_count, head_count = totals.shape
    return (
        (sums.reshape(row_count, head_count, -1) / totals[..., None])
        .reshape(row_count, -1)
        .astype(jnp.bfloat16)
    )


def attend_own(query_rows, row_start, keys_new, values_new, span_len):
    query_count = query_rows.shape[0]
    rows_each = min(query_count, span_len)
    blocks = max(query_count // span_len, 1)
    pieces = []
    for block_index in range(blocks):
        first_row = row_start + block_index * rows_each
        key_start = first_row // span_len * span_len
        block_keys = lax.dynamic_slice_in_dim(keys_new, key_start, span_len, 0)
        block_values = lax.dynamic_slice_in_dim(values_new, key_start, span_len, 0)
        allowed = (
            first_row - key_start + jnp.arange(rows_each)[:, None] >= jnp.arange(span_len)[None, :]
        )
        block_rows = query_rows[block_index * rows_each : (block_index + 1) * rows_each]
        pieces.append(partial_block(block_rows, block_keys, block_values, allowed))
    return tuple(
        (
            jnp.concatenate([block_terms[member] for block_terms in pieces], axis=0)
            for member in range(3)
        )
    )


def per_device(query_in, key_in, value_in, cache_keys, cache_values, live_slots, span_starts):
    devices = lax.axis_size("kv")
    device_index = lax.axis_index("kv")
    share_rows = query_in.shape[0]
    token_count = share_rows * devices
    span_count = span_starts.shape[0]
    span_len = token_count // span_count
    head_size = HD
    head_count = query_in.shape[1] // head_size
    kv_heads = key_in.shape[1] // head_size
    row_start = device_index * share_rows
    positions = (span_starts[:, None] + jnp.arange(span_len, dtype=jnp.int32)[None, :]).reshape(
        token_count
    )
    full_query, full_key, full_value = (
        lax.all_gather(query_in, "kv", axis=0, tiled=True),
        lax.all_gather(key_in, "kv", axis=0, tiled=True),
        lax.all_gather(value_in, "kv", axis=0, tiled=True),
    )
    queries = rotate_pairs(
        full_query.astype(jnp.float32).reshape(token_count, head_count, head_size), positions
    ).astype(jnp.bfloat16)
    keys_new = rotate_pairs(
        full_key.astype(jnp.float32).reshape(token_count, kv_heads, head_size), positions
    ).astype(jnp.bfloat16)
    values_new = full_value.reshape(token_count, kv_heads, head_size)
    slot_count = cache_keys.shape[1]
    slot_index = jnp.arange(slot_count)
    partials = []
    for span_index in range(span_count):
        query_rows = queries[span_index * span_len : (span_index + 1) * span_len]
        allowed = (slot_index < live_slots[span_index, 0])[None, :]
        block_keys = cache_keys[span_index].reshape(slot_count, kv_heads, head_size)
        block_values = cache_values[span_index].reshape(slot_count, kv_heads, head_size)
        partials.append(partial_block(query_rows, block_keys, block_values, allowed))
    local_max, local_total, local_sum = tuple(
        (
            jnp.concatenate([block_terms[member] for block_terms in partials], axis=0)
            for member in range(3)
        )
    )
    global_max = lax.pmax(local_max, "kv")
    scaled_total, scaled_sum = rescale(local_max, local_total, local_sum, global_max)
    total_all, sum_all = lax.psum((scaled_total, scaled_sum), "kv")
    own_terms = attend_own(queries, 0, keys_new, values_new, span_len)
    attended = normalize(fold_pair((global_max, total_all, sum_all), own_terms))
    return lax.dynamic_slice_in_dim(attended, row_start, share_rows, 0)


def solution(mesh):
    in_specs = (
        P(("groups", "kv"), None),
        P(("groups", "kv"), None),
        P(("groups", "kv"), None),
        P("groups", "kv", None),
        P("groups", "kv", None),
        P("groups", "kv"),
        P("groups"),
    )
    out_specs = P(("groups", "kv"), None)
    return jax.shard_map(
        per_device, mesh=mesh, in_specs=in_specs, out_specs=out_specs, check_vma=False
    )
```

profile of v0, /device:TPU:0, one launch (start us, length us, event | category | flops | bytes accessed | tf_op | source)
XLA Modules:
  0.0 184.7 jit_solution(2079144054091446826)
XLA Ops:
  6.5 0.7 iota_add_fusion
  7.3 24.8 %all_gather.9 = bf16[128,2048]{1,0:T(8,128)(2,1)S(1)} all-gather(bf16[8,2048]{1,0:T(8,128)(2,1)} %param.9), channel_id=1, replica_groups=mesh['groups'=2,'kv'=16] {'kv'}, dimensions={0}, use_global_device_ids=true | all-gather | bytes 557056 | tf_op jit(solution)/shard_map/all_gather | solution.py:138
  33.1 0.6 fusion.64
  33.7 0.6 iota_compare_fusion.2
  34.4 0.9 copy.92
  35.4 1.1 iota_compare_fusion.1
  36.5 0.9 copy.94
  37.8 0.7 add_convert_fusion
  38.8 0.6 copy-done.2
  40.4 0.7 pad_maximum_fusion.2
  41.1 31.0 %pmax.7 = f32[128,16]{0,1:T(8,128)} all-reduce(f32[128,16]{0,1:T(8,128)} %pad_maximum_fusion.2), channel_id=1, replica_groups=mesh['groups'=2,'kv'=16] {'kv'}, use_global_device_ids=true, to_apply=%region_2.3 | all-reduce | flops 2048 | bytes 16384 | tf_op jit(solution)/shard_map/pmax | solution.py:164
  72.1 1.1 fusion.4
  73.8 0.7 maximum_multiply_fusion
  74.5 1.4 copy.55
  75.9 2.1 %fusion.60 = (bf16[1,384,512]{2,1,0:T(8,128)(2,1)}, bf16[1,384,512]{2,1,0:T(8,128)(2,1)}) fusion(bf16[2,384,512]{2,1,0:T(8,128)(2,1)} %param.13), kind=kLoop, calls=%fused_computation.96 | loop fusion | bytes 1572864 | tf_op jit(solution)/shard_map/slice | solution.py:156
  77.9 1.9 %copy.93 = bf16[1,384,512]{1,2,0:T(8,128)(2,1)} copy(bf16[1,384,512]{2,1,0:T(8,128)(2,1)} %get-tuple-element.18) | data formatting | bytes 786432
  79.9 1.4 convolution_bitcast_fusion.3
  84.1 1.5 bitcast_multiply_fusion
  85.7 17.8 %all_gather.10 = bf16[128,512]{1,0:T(8,128)(2,1)S(1)} all-gather(bf16[8,512]{1,0:T(8,128)(2,1)S(1)} %copy-done.10), channel_id=1, replica_groups=mesh['groups'=2,'kv'=16] {'kv'}, dimensions={0}, use_global_device_ids=true | all-gather | bytes 139264 | tf_op jit(solution)/shard_map/all_gather | solution.py:139
  104.8 32.1 %psum.15 = f32[128,16]{0,1:T(8,128)S(1)} all-reduce(f32[128,16]{0,1:T(8,128)S(1)} %copy-done.9), channel_id=1, replica_groups=mesh['groups'=2,'kv'=16] {'kv'}, use_global_device_ids=true, to_apply=%region_8.9 | all-reduce | flops 2048 | bytes 16384 | tf_op jit(solution)/shard_map/psum | solution.py:166
  138.3 17.9 %all_gather.11 = bf16[128,512]{1,0:T(8,128)(2,1)S(1)} all-gather(bf16[8,512]{1,0:T(8,128)(2,1)S(1)} %copy-done.11), channel_id=1, replica_groups=mesh['groups'=2,'kv'=16] {'kv'}, dimensions={0}, use_global_device_ids=true | all-gather | bytes 139264 | tf_op jit(solution)/shard_map/all_gather | solution.py:140
  158.7 1.9 %copy_bitcast_fusion = (f32[128,2048]{1,0:T(8,128)S(1)}, f32[128,2048]{1,0:T(8,128)}) fusion(f32[16,8,16,128]{3,2,1,0:T(8,128)S(1)} %bitcast.134, f32[16,8,16,128]{3,2,1,0:T(8,128)S(1)} %bitcast.133), kind=kLoop, calls=%fused_computation.24 | loop fusion | bytes 4194304 | tf_op jit(solution)/shard_map/div | solution.py:94
  160.5 15.8 %all-reduce.2.cloned.1.call-done = f32[128,2048]{1,0:T(8,128)} async-done(((f32[128,2048]{1,0:T(8,128)}), f32[128,2048]{1,0:T(8,128)}) %all-reduce.2.cloned.1.call-update) | async-done | bytes 1048592 | tf_op jit(solution)/shard_map/psum | solution.py:166
  176.3 1.5 fusion.47
  (80 shorter events, 11.0 us)
Async XLA Ops:
  6.5 169.8 %all-reduce.2.cloned.1.call-start = ((), (), s32[]{:S(2)}) async-start(), calls=%async_computation | async-start | bytes 2097152 | tf_op jit(solution)/shard_map/psum | solution.py:166
  32.4 0.7 copy-start.16
  32.4 1.9 %copy-start.5 = (bf16[2,384,512]{2,1,0:T(8,128)(2,1)S(1)}, bf16[2,384,512]{2,1,0:T(8,128)(2,1)}, u32[]{:S(2)}) copy-start(bf16[2,384,512]{2,1,0:T(8,128)(2,1)} %param.12) | copy-start | bytes 2359300
  34.4 4.5 %copy-start.15 = (pred[384]{0:T(512)(128)(4,1)}, pred[384]{0:T(512)(128)(4,1)S(1)}, u32[]{:S(2)}) copy-start(pred[384]{0:T(512)(128)(4,1)S(1)} %iota_compare_fusion.2) | copy-start | bytes 1156
  34.4 3.1 %copy-start.17 = (s32[64]{0:T(128)S(1)}, s32[64]{0:T(128)}, u32[]{:S(2)}) copy-start(s32[64]{0:T(128)} %constant.9.clone) | copy-start | bytes 772
  38.5 1.0 copy-start.2
  38.5 1.4 copy-start.3
  38.5 1.4 copy-start.12
  38.8 1.6 copy-start
  72.1 1.2 copy-start.13
  72.1 1.7 copy-start.7
  81.3 1.0 copy-start.4
  81.3 1.2 copy-start.14
  82.9 0.8 copy-start.6
  84.1 1.6 copy-start.10
  85.6 18.3 %copy-start.1 = (bf16[64,16,128]{2,0,1:T(8,128)(2,1)S(1)}, bf16[64,16,128]{2,0,1:T(8,128)(2,1)}, u32[]{:S(2)}) copy-start(bf16[64,16,128]{2,0,1:T(8,128)(2,1)} %copy-done) | copy-start | bytes 786436
  103.9 1.0 copy-start.9
  104.0 33.3 %copy-start.8 = (f32[128,16]{0,1:T(8,128)S(1)}, f32[128,16]{0,1:T(8,128)}, u32[]{:S(2)}) copy-start(f32[128,16]{0,1:T(8,128)} %pmax.7) | copy-start | bytes 24580
  137.6 0.7 copy-start.11
Sparse Core Ops, SparseCore 0:
  85.8 90.5 all-reduce.1
where the time goes:
time: 185 us
  blocking collectives  124 us (67%)
  local copies, waits for them, and re-layouts  17 us (9%)
  waiting for transfers between devices  15.8 us (9%)
  between operations  13.9 us (8%)
  other arithmetic  10.4 us (6%)
  matrix products  4.15 us (2%)
    psum x1, blocking collectives, per_device(): total_all, sum_all = lax.psum((scaled_total, scaled_sum), 'kv')  32.1 us
    pmax x1, blocking collectives, per_device(): global_max = lax.pmax(local_max, 'kv')  31 us
    all_gather x1, blocking collectives, per_device(): lax.all_gather(query_in, 'kv', axis=0, tiled=True)  24.8 us
    all_gather x1, blocking collectives, per_device(): lax.all_gather(value_in, 'kv', axis=0, tiled=True)  17.9 us
    all_gather x1, blocking collectives, per_device(): lax.all_gather(key_in, 'kv', axis=0, tiled=True)  17.8 us
    psum x1, waiting for transfers between devices, per_device(): total_all, sum_all = lax.psum((scaled_total, scaled_sum), 'kv')  15.8 us
    unnamed x44, local copies, waits for them, and re-layouts  6.49 us
  transfers between devices with their start and end apart: 1, of which 1 were waited for; matrix products, arithmetic and copies ran while one was open for 4% of the time, Pallas kernels for 0%

commit v1 on v0

--- a/solution.py
+++ b/solution.py
@@ -1,13 +1,20 @@
+import functools
+import math
+
 import jax
 import jax.numpy as jnp
 import numpy as np
 from jax import lax
+from jax.experimental import pallas as pl
+from jax.experimental.pallas import tpu as pltpu
 from jax.sharding import PartitionSpec as P
 
 HD = 128
 
 
 NEG_FILL = -1e30
+NEG_FLOOR = -1e29
+MESH = pl.DeviceIdType.MESH
 
 
 def turn_table(head_size):
@@ -169,6 +176,345 @@
     return lax.dynamic_slice_in_dim(attended, row_start, share_rows, 0)
 
 
+def flip_bits(index, mask):
+    result = index
+    bit = 1
+    while bit <= mask:
+        if mask & bit:
+            result = result + bit * (1 - 2 * lax.rem(lax.div(index, bit), 2))
+        bit *= 2
+    return result
+
+
+def attend_kernel(
+    devices, span_count, kv_heads, group_size,
+    turn_ref, query_ref, key_ref, value_ref, cache_k, cache_v, live_ref, start_ref, out_ref,
+    q_slots, q_other, k_buf, v_buf, new_send, new_recv, live_send, live_recv,
+    o_send, o_recv, s_send, s_recv,
+    q_ssem, q_rsem, o_ssem, o_rsem, s_ssem, s_rsem, cache_ssem, cache_rsem, local_sem,
+    misc_ssem, misc_rsem,
+):
+    share = query_ref.shape[0]
+    slots = cache_k.shape[1]
+    half_kv = kv_heads // 2
+    half_heads = half_kv * group_size
+    half_lanes = half_kv * HD
+    span_devices = devices // span_count
+    span_len = share * span_devices
+    scale2 = HD ** (-0.5) * math.log2(math.e)
+
+    me = lax.axis_index("kv")
+    half = lax.rem(me, 2)
+    near = lax.div(me, span_devices)
+
+    def target(mask):
+        return {"kv": flip_bits(me, mask)}
+
+    def lanes(which, width):
+        return pl.ds(pl.multiple_of(which * width, 128), width)
+
+    local_copies = []
+    for order in range(span_count):
+        span = flip_bits(near, order)
+        for which, (src, dst) in enumerate(((cache_k, k_buf), (cache_v, v_buf))):
+            copy = pltpu.make_async_copy(
+                src.at[span, :, lanes(half, half_lanes)],
+                dst.at[order, pl.ds(0, slots)],
+                local_sem.at[order, which],
+            )
+            copy.start()
+            local_copies.append(copy)
+
+    barrier = pltpu.get_barrier_semaphore()
+    for mask in range(1, devices):
+        pl.semaphore_signal(barrier, inc=1, device_id=target(mask), device_id_type=MESH)
+
+    first_token = me * share
+    position = (
+        start_ref[near]
+        + (first_token - near * span_len)
+        + lax.broadcasted_iota(jnp.int32, (share, HD), 0)
+    )
+    angles = (position * turn_ref[...]).astype(jnp.float32) * (2.0 * np.pi / 2.0**32)
+    cosine = jnp.cos(angles)
+    lane = lax.broadcasted_iota(jnp.int32, (share, HD), 1)
+    sine = jnp.sin(angles)
+    sine = jnp.where(lane < HD // 2, -sine, sine)
+
+    def rotated(ref, offset):
+        x = ref[:, pl.ds(pl.multiple_of(offset, 128), HD)].astype(jnp.float32)
+        return x * cosine + pltpu.roll(x, HD // 2, 1) * sine
+
+    for which, dst in ((half, q_slots.at[0]), (1 - half, q_other)):
+        for head in range(0, half_heads, 2):
+            offset = which * (half_heads * HD) + head * HD
+            pair = jnp.concatenate(
+                [rotated(query_ref, offset), rotated(query_ref, offset + HD)], axis=0
+            )
+            dst[head * share : (head + 2) * share, :] = pair.astype(jnp.bfloat16)
+
+    def new_rows(which):
+        keys = jnp.concatenate(
+            [rotated(key_ref, which * half_lanes + g * HD) for g in range(half_kv)], axis=1
+        )
+        values = value_ref[:, lanes(which, half_lanes)].astype(jnp.float32)
+        return keys, values
+
+    other_keys, other_values = new_rows(1 - half)
+    new_send[...] = jnp.concatenate([other_keys, other_values], axis=0).astype(jnp.bfloat16)
+    own_keys, own_values = new_rows(half)
+    live_row = lax.broadcasted_iota(jnp.int32, live_send.shape, 0)
+    live_tile = jnp.zeros(live_send.shape, jnp.int32)
+    for order in range(span_count):
+        live_tile = jnp.where(live_row == order, live_ref[flip_bits(near, order), 0], live_tile)
+    live_send[...] = live_tile
+
+    pl.semaphore_wait(barrier, devices - 1)
+
+    def remote(src, dst, ssem, rsem, mask):
+        return pltpu.make_async_remote_copy(
+            src_ref=src, dst_ref=dst, send_sem=ssem, recv_sem=rsem,
+            device_id=target(mask), device_id_type=MESH,
+        )
+
+    q_copies = {}
+    for mask in range(1, devices):
+        src = q_slots.at[0] if mask % 2 == 0 else q_other
+        q_copies[mask] = remote(src, q_slots.at[mask], q_ssem.at[mask], q_rsem.at[mask], mask)
+    for mask in range(devices - 1, span_devices - 1, -1):
+        q_copies[mask].start()
+    for mask in range(1, span_devices):
+        q_copies[mask].start()
+    cache_copies = {}
+    for order in range(span_count):
+        span = flip_bits(near, order)
+        for which, (src, dst) in enumerate(((cache_k, k_buf), (cache_v, v_buf))):
+            copy = remote(
+                src.at[span, :, lanes(1 - half, half_lanes)],
+                dst.at[order, pl.ds(slots, slots)],
+                cache_ssem.at[order, which], cache_rsem.at[order, which], 1,
+            )
+            copy.start()
+            cache_copies[order, which] = copy
+        if order == 0:
+            new_copy = remote(new_send, new_recv, misc_ssem.at[0], misc_rsem.at[0], 1)
+            new_copy.start()
+            live_copy = remote(live_send, live_recv, misc_ssem.at[1], misc_rsem.at[1], 1)
+            live_copy.start()
+
+    stat_lane = lax.broadcasted_iota(jnp.int32, (share, HD), 1)
+    group_rows = group_size * share
+    o_copies = []
+
+    for order in range(span_count):
+        first_slot = order * span_devices
+        for mask in range(max(first_slot, 1), first_slot + span_devices):
+            q_copies[mask].wait_recv()
+        if order == 0:
+            new_copy.wait_recv()
+            live_copy.wait_recv()
+        local_copies[2 * order].wait()
+        local_copies[2 * order + 1].wait()
+        cache_copies[order, 0].wait_recv()
+        cache_copies[order, 1].wait_recv()
+
+        column = lax.broadcasted_iota(jnp.int32, (1, slots), 1)
+        own_live = live_ref[flip_bits(near, order), 0]
+        peer_live = jnp.broadcast_to(live_recv[order : order + 1, 0:1], (1, slots))
+        bias = jnp.concatenate(
+            [
+                jnp.where(column < own_live, 0.0, NEG_FILL),
+                jnp.where(column < peer_live, 0.0, NEG_FILL),
+            ],
+            axis=1,
+        )
+        row_total = span_devices * group_rows
+        if order == 0:
+            filler = jnp.zeros((HD - 2 * share, half_lanes), jnp.float32)
+            received = new_recv[...].astype(jnp.float32)
+            new_keys = jnp.concatenate(
+                [own_keys, received[:share], filler], axis=0
+            ).astype(jnp.bfloat16)
+            new_values = jnp.concatenate(
+                [own_values, received[share:], filler], axis=0
+            ).astype(jnp.bfloat16)
+            pieces = []
+            key_column = lax.broadcasted_iota(jnp.int32, (share, HD), 1)
+            token_row = lax.broadcasted_iota(jnp.int32, (share, HD), 0)
+            key_token = jnp.where(
+                key_column < share,
+                first_token + key_column,
+                flip_bits(me, 1) * share + key_column - share,
+            )
+            for mask in range(span_devices):
+                admitted = (key_column < 2 * share) & (
+                    key_token <= flip_bits(me, mask) * share + token_row
+                )
+                piece = jnp.where(admitted, 0.0, NEG_FILL)
+                pieces.extend([piece] * group_size)
+            new_bias = jnp.concatenate(pieces, axis=0)
+
+        stats = [jnp.zeros((share, HD), jnp.float32) for unused in range(span_devices)]
+        for g in range(half_kv):
+            queries = q_slots[
+                first_slot : first_slot + span_devices, g * group_rows : (g + 1) * group_rows, :
+            ].reshape(row_total, HD)
+            head_lanes = slice(g * HD, (g + 1) * HD)
+            nt = (((1,), (1,)), ((), ()))
+            scores = lax.dot_general(
+                queries, k_buf[order, :, head_lanes], nt, preferred_element_type=jnp.float32
+            ) + bias
+            maxima = jnp.max(scores, axis=1, keepdims=True)
+            if order == 0:
+                new_scores = lax.dot_general(
+                    queries, new_keys[:, head_lanes], nt, preferred_element_type=jnp.float32
+                ) + new_bias
+                maxima = jnp.maximum(maxima, jnp.max(new_scores, axis=1, keepdims=True))
+            maxima = jnp.maximum(maxima, NEG_FLOOR)
+            weights = jnp.exp2((scores - maxima) * scale2)
+            totals = jnp.sum(weights, axis=1, keepdims=True)
+            sums = jnp.dot(
+                weights.astype(jnp.bfloat16), v_buf[order, :, head_lanes],
+                preferred_element_type=jnp.float32,
+            )
+            if order == 0:
+                new_weights = jnp.exp2((new_scores - maxima) * scale2)
+                totals = totals + jnp.sum(new_weights, axis=1, keepdims=True)
+                sums = sums + jnp.dot(
+                    new_weights.astype(jnp.bfloat16), new_values[:, head_lanes],
+                    preferred_element_type=jnp.float32,
+                )
+            o_send[
+                first_slot : first_slot + span_devices, g * group_rows : (g + 1) * group_rows, :
+            ] = sums.astype(jnp.bfloat16).reshape(span_devices, group_rows, HD)
+            for member in range(span_devices):
+                for h in range(group_size):
+                    begin = member * group_rows + h * share
+                    where = g * group_size + h
+                    stats[member] = jnp.where(
+                        stat_lane == where, maxima[begin : begin + share], stats[member]
+                    )
+                    stats[member] = jnp.where(
+                        stat_lane == where + HD // 2, totals[begin : begin + share], stats[member]
+                    )
+        for member in range(span_devices):
+            s_send[first_slot + member] = stats[member]
+        for member in reversed(range(span_devices)):
+            mask = first_slot + member
+            if mask == 0:
+                continue
+            for src, dst, ssem, rsem in (
+                (s_send, s_recv, s_ssem, s_rsem),
+                (o_send, o_recv, o_ssem, o_rsem),
+            ):
+                copy = remote(src.at[mask], dst.at[mask], ssem.at[mask], rsem.at[mask], mask)
+                copy.start()
+                o_copies.append(copy)
+
+    for copy in o_copies:
+        copy.wait_recv()
+
+    for parity in range(2):
+        masks = list(range(parity, devices, 2))
+        stat = [s_send[0] if mask == 0 else s_recv[mask] for mask in masks]
+        top = functools.reduce(jnp.maximum, stat)
+        factors = [jnp.exp2((s - top) * scale2) for s in stat]
+        total = functools.reduce(
+            jnp.add, [f * pltpu.roll(s, HD // 2, 1) for f, s in zip(factors, stat)]
+        )
+        inverse = 1.0 / total
+        accumulated = [None] * half_heads
+        for f, mask in zip(factors, masks):
+            weight = f * inverse
+            block = (o_send[0] if mask == 0 else o_recv[mask]).astype(jnp.float32)
+            for head in range(half_heads):
+                term = weight[:, head : head + 1] * block[head * share : (head + 1) * share]
+                accumulated[head] = (
+                    term if accumulated[head] is None else accumulated[head] + term
+                )
+        which = half if parity == 0 else 1 - half
+        out_ref[:, lanes(which, half_heads * HD)] = jnp.concatenate(
+            accumulated, axis=1
+        ).astype(jnp.bfloat16)
+
+    for copy in list(q_copies.values()) + list(cache_copies.values()) + o_copies:
+        copy.wait_send()
+    new_copy.wait_send()
+    live_copy.wait_send()
+
+
+def fused_device(query_in, key_in, value_in, cache_keys, cache_values, live_slots, span_starts):
+    devices = lax.axis_size("kv")
+    share = query_in.shape[0]
+    spans, slots, kv_width = cache_keys.shape
+    kv_heads = kv_width // HD
+    group_size = query_in.shape[1] // kv_width
+    half_kv = kv_heads // 2
+    rows = half_kv * group_size * share
+    turns = jnp.concatenate([turn_table(HD)] * 2)[None, :]
+    vmem = pl.BlockSpec(memory_space=pltpu.VMEM)
+    smem = pl.BlockSpec(memory_space=pltpu.SMEM)
+    hbm = pl.BlockSpec(memory_space=pl.ANY)
+    dma = pltpu.SemaphoreType.DMA
+    bf16 = jnp.bfloat16
+    return pl.pallas_call(
+        functools.partial(attend_kernel, devices, spans, kv_heads, group_size),
+        out_shape=jax.ShapeDtypeStruct(query_in.shape, bf16),
+        in_specs=[vmem, vmem, vmem, vmem, hbm, hbm, smem, smem],
+        out_specs=vmem,
+        scratch_shapes=[
+            pltpu.VMEM((devices, rows, HD), bf16),
+            pltpu.VMEM((rows, HD), bf16),
+            pltpu.VMEM((spans, 2 * slots, half_kv * HD), bf16),
+            pltpu.VMEM((spans, 2 * slots, half_kv * HD), bf16),
+            pltpu.VMEM((2 * share, half_kv * HD), bf16),
+            pltpu.VMEM((2 * share, half_kv * HD), bf16),
+            pltpu.VMEM((8, HD), jnp.int32),
+            pltpu.VMEM((8, HD), jnp.int32),
+            pltpu.VMEM((devices, rows, HD), bf16),
+            pltpu.VMEM((devices, rows, HD), bf16),
+            pltpu.VMEM((devices, share, HD), jnp.float32),
+            pltpu.VMEM((devices, share, HD), jnp.float32),
+            dma((devices,)), dma((devices,)), dma((devices,)), dma((devices,)),
+            dma((devices,)), dma((devices,)),
+            dma((spans, 2)), dma((spans, 2)), dma((spans, 2)),
+            dma((2,)), dma((2,)),
+        ],
+        compiler_params=pltpu.CompilerParams(
+            collective_id=0, has_side_effects=True, vmem_limit_bytes=40 * 2**20
+        ),
+        name="fused_attention",
+    )(turns, query_in, key_in, value_in, cache_keys, cache_values, live_slots, span_starts)
+
+
+def is_power(number):
+    return number > 0 and number & (number - 1) == 0
+
+
+def fits_kernel(query_in, key_in, cache_keys, span_starts):
+    devices = lax.axis_size("kv")
+    spans = span_starts.shape[0]
+    kv_heads = key_in.shape[1] // HD
+    return (
+        is_power(devices)
+        and is_power(spans)
+        and devices >= 2 * spans
+        and query_in.shape[0] == 8
+        and kv_heads % 2 == 0
+        and query_in.shape[1] % key_in.shape[1] == 0
+        and cache_keys.shape[1] % 128 == 0
+        and spans <= 8
+        and kv_heads // 2 * (query_in.shape[1] // key_in.shape[1]) <= 64
+    )
+
+
+def one_device(query_in, key_in, value_in, cache_keys, cache_values, live_slots, span_starts):
+    arrays = (query_in, key_in, value_in, cache_keys, cache_values, live_slots, span_starts)
+    if fits_kernel(query_in, key_in, cache_keys, span_starts):
+        return fused_device(*arrays)
+    return per_device(*arrays)
+
+
 def solution(mesh):
     in_specs = (
         P(("groups", "kv"), None),
@@ -181,5 +527,5 @@
     )
     out_specs = P(("groups", "kv"), None)
     return jax.shard_map(
-        per_device, mesh=mesh, in_specs=in_specs, out_specs=out_specs, check_vma=False
-    )
+        one_device, mesh=mesh, in_specs=in_specs, out_specs=out_specs, check_vma=False
+    )

time: 185 us -> 31.4 us (0.17)
  blocking collectives: 124 us -> 0 us
  Pallas kernels: 0 us -> 25.2 us
  waiting for transfers between devices: 15.8 us -> 0 us
  between operations: 13.9 us -> 0.02 us
  local copies, waits for them, and re-layouts: 17 us -> 5.81 us
  other arithmetic: 10.4 us -> 0 us
  matrix products: 4.15 us -> 0 us
    all_gather x3 -> x0, blocking collectives: 60.4 us -> none  [the longest x1 24.8 us: per_device(): lax.all_gather(query_in, 'kv', axis=0, tiled=True)]
    psum x1 -> x0, blocking collectives: 32.1 us -> none  [per_device(): total_all, sum_all = lax.psum((scaled_total, scaled_sum), 'kv')]
    pmax x1 -> x0, blocking collectives: 31 us -> none  [per_device(): global_max = lax.pmax(local_max, 'kv')]
    pallas_call x0 -> x1, Pallas kernels: none -> 25.2 us  [fused_device(): pl.pallas_call(functools.partial(attend_kernel, devices, spans, kv_heads,...]
    psum x1 -> x0, waiting for transfers between devices: 15.8 us -> none  [per_device(): total_all, sum_all = lax.psum((scaled_total, scaled_sum), 'kv')]
    dot_general x8 -> x0, matrix products: 4.15 us -> none  [the longest x4 2.42 us: partial_block(): jnp.einsum('kgrs,skd->rkgd', weights.astype(jnp.bfloat16), block_values,...]
    slice x5 -> x0, local copies, waits for them, and re-layouts: 3.08 us -> none  [the longest x1 2.06 us: per_device(): cache_values[span_index].reshape(slot_count, kv_heads, head_size)]
    div x2 -> x0, local copies, waits for them, and re-layouts: 2.22 us -> none  [normalize(): sums.reshape(row_count, head_count, -1) / totals[..., None]]
  transfers between devices with their start and end apart: 1 -> 0, of which waited for: 1 -> 0; matrix products, arithmetic and copies ran while one was open for 4% -> 0% of each run, Pallas kernels for 0% -> 0%
where the time goes in v1:
time: 31.4 us; the launch traced here: 31.1 us
  Pallas kernels  25.2 us (80%)
  local copies, waits for them, and re-layouts  5.81 us (19%)
    pallas_call x1, Pallas kernels, fused_device(): pl.pallas_call(functools.partial(attend_kernel, devices, spans, kv_heads,...  25.2 us
    unnamed x16, local copies, waits for them, and re-layouts  5.81 us

profile of v1, /device:TPU:0, one launch (start us, length us, event | category | flops | bytes accessed | tf_op | source)
XLA Modules:
  0.0 31.1 jit_solution(8091755033167380092)
XLA Ops:
  0.0 0.0 copy-start.6
  0.0 0.0 copy-start.5
  0.0 0.8 %copy.9.live_ref = s32[2,1]{1,0:T(2,128)S(1)} copy(s32[2,1]{0,1:T(1,128)} %param.13) | data formatting | bytes 16 | tf_op args[5]
  0.8 0.0 copy-done.6
  0.8 0.0 copy-done.5
  0.8 0.0 copy-start
  0.8 1.1 %copy-done = bf16[2,384,512]{2,1,0:T(8,128)(2,1)S(1)} copy-done((bf16[2,384,512]{2,1,0:T(8,128)(2,1)S(1)}, bf16[2,384,512]{2,1,0:T(8,128)(2,1)}, u32[]{:S(2)}) %copy-start) | copy-done | bytes 786456
  1.9 0.0 copy-start.1
  1.9 1.1 %copy-done.1 = bf16[2,384,512]{2,1,0:T(8,128)(2,1)S(1)} copy-done((bf16[2,384,512]{2,1,0:T(8,128)(2,1)S(1)}, bf16[2,384,512]{2,1,0:T(8,128)(2,1)}, u32[]{:S(2)}) %copy-start.1) | copy-done | bytes 786456
  3.0 0.0 copy-start.2
  3.0 0.8 %copy-done.2 = bf16[8,2048]{1,0:T(8,128)(2,1)S(1)} copy-done((bf16[8,2048]{1,0:T(8,128)(2,1)S(1)}, bf16[8,2048]{1,0:T(8,128)(2,1)}, u32[]{:S(2)}) %copy-start.2) | copy-done | bytes 32792
  3.8 0.0 copy-start.3
  3.8 0.7 %copy-done.3 = bf16[8,512]{1,0:T(8,128)(2,1)S(1)} copy-done((bf16[8,512]{1,0:T(8,128)(2,1)S(1)}, bf16[8,512]{1,0:T(8,128)(2,1)}, u32[]{:S(2)}) %copy-start.3) | copy-done | bytes 8216
  4.5 0.0 copy-start.4
  4.5 0.7 %copy-done.4 = bf16[8,512]{1,0:T(8,128)(2,1)S(1)} copy-done((bf16[8,512]{1,0:T(8,128)(2,1)S(1)}, bf16[8,512]{1,0:T(8,128)(2,1)}, u32[]{:S(2)}) %copy-start.4) | copy-done | bytes 8216
  5.2 25.2 %fused_attention.1 = bf16[8,2048]{1,0:T(8,128)(2,1)S(1)} custom-call(s32[1,128]{1,0:T(1,128)S(1)} %copy-done.6, bf16[8,2048]{1,0:T(8,128)(2,1)S(1)} %copy-done.2, bf16[8,512]{1,0:T(8,128)(2,1)S(1)} %copy-done.3, bf16[8,512]{1,0:T(8,128)(2,1)S(1)} %copy-done.4, bf16[2,384,512]{2,1,0:T(8,128)(2,1)S(1)} %copy-done, bf16[2,384,512]{2,1,0:T(8,128)(2,1)S(1)} %copy-done.1, ...), custom_call_target="tpu_custom_call" | custom-call | tf_op jit(solution)/shard_map/fused_attention/pallas_call | solution.py:460
  30.4 0.6 %copy.11 = bf16[8,2048]{1,0:T(8,128)(2,1)} copy(bf16[8,2048]{1,0:T(8,128)(2,1)S(1)} %fused_attention.1) | data formatting | bytes 65536
Async XLA Ops:
  0.0 0.8 %copy-start.6 = (s32[1,128]{1,0:T(1,128)S(1)}, s32[1,128]{1,0:T(1,128)}, u32[]{:S(2)}) copy-start(s32[1,128]{1,0:T(1,128)} %constant.8.turn_ref) | copy-start | bytes 1540
  0.0 0.8 %copy-start.5 = (s32[2]{0:T(128)S(1)}, s32[2]{0:T(128)}, u32[]{:S(2)}) copy-start(s32[2]{0:T(128)} %start_ref.1) | copy-start | bytes 28
  0.8 1.1 %copy-start = (bf16[2,384,512]{2,1,0:T(8,128)(2,1)S(1)}, bf16[2,384,512]{2,1,0:T(8,128)(2,1)}, u32[]{:S(2)}) copy-start(bf16[2,384,512]{2,1,0:T(8,128)(2,1)} %cache_k.1) | copy-start | bytes 2359300
  1.9 1.1 %copy-start.1 = (bf16[2,384,512]{2,1,0:T(8,128)(2,1)S(1)}, bf16[2,384,512]{2,1,0:T(8,128)(2,1)}, u32[]{:S(2)}) copy-start(bf16[2,384,512]{2,1,0:T(8,128)(2,1)} %cache_v.1) | copy-start | bytes 2359300
  3.0 0.8 %copy-start.2 = (bf16[8,2048]{1,0:T(8,128)(2,1)S(1)}, bf16[8,2048]{1,0:T(8,128)(2,1)}, u32[]{:S(2)}) copy-start(bf16[8,2048]{1,0:T(8,128)(2,1)} %query_ref.1) | copy-start | bytes 98308
  3.8 0.7 %copy-start.3 = (bf16[8,512]{1,0:T(8,128)(2,1)S(1)}, bf16[8,512]{1,0:T(8,128)(2,1)}, u32[]{:S(2)}) copy-start(bf16[8,512]{1,0:T(8,128)(2,1)} %key_ref.1) | copy-start | bytes 24580
  4.5 0.7 %copy-start.4 = (bf16[8,512]{1,0:T(8,128)(2,1)S(1)}, bf16[8,512]{1,0:T(8,128)(2,1)}, u32[]{:S(2)}) copy-start(bf16[8,512]{1,0:T(8,128)(2,1)} %value_ref.1) | copy-start | bytes 24580

commit v2 on v1

--- a/solution.py
+++ b/solution.py
@@ -188,13 +188,14 @@
 
 def attend_kernel(
     devices, span_count, kv_heads, group_size,
-    turn_ref, query_ref, key_ref, value_ref, cache_k, cache_v, live_ref, start_ref, out_ref,
+    turn_hbm, query_hbm, key_hbm, value_hbm, cache_k, cache_v, live_hbm, start_hbm, out_ref,
+    turn_ref, query_ref, key_ref, value_ref, live_ref, start_ref, in_sem,
     q_slots, q_other, k_buf, v_buf, new_send, new_recv, live_send, live_recv,
     o_send, o_recv, s_send, s_recv,
     q_ssem, q_rsem, o_ssem, o_rsem, s_ssem, s_rsem, cache_ssem, cache_rsem, local_sem,
     misc_ssem, misc_rsem,
 ):
-    share = query_ref.shape[0]
+    share = query_hbm.shape[0]
     slots = cache_k.shape[1]
     half_kv = kv_heads // 2
     half_heads = half_kv * group_size
@@ -212,6 +213,21 @@
 
     def lanes(which, width):
         return pl.ds(pl.multiple_of(which * width, 128), width)
+
+    barrier = pltpu.get_barrier_semaphore()
+    for mask in range(1, devices):
+        pl.semaphore_signal(barrier, inc=1, device_id=target(mask), device_id_type=MESH)
+
+    operand_copies = []
+    for index, (src, dst) in enumerate(
+        (
+            (start_hbm, start_ref), (turn_hbm, turn_ref), (query_hbm, query_ref),
+            (key_hbm, key_ref), (value_hbm, value_ref), (live_hbm, live_ref),
+        )
+    ):
+        copy = pltpu.make_async_copy(src, dst, in_sem.at[index])
+        copy.start()
+        operand_copies.append(copy)
 
     local_copies = []
     for order in range(span_count):
@@ -225,10 +241,8 @@
             copy.start()
             local_copies.append(copy)
 
-    barrier = pltpu.get_barrier_semaphore()
-    for mask in range(1, devices):
-        pl.semaphore_signal(barrier, inc=1, device_id=target(mask), device_id_type=MESH)
-
+    for copy in operand_copies:
+        copy.wait()
     first_token = me * share
     position = (
         start_ref[near]
@@ -266,7 +280,7 @@
     live_row = lax.broadcasted_iota(jnp.int32, live_send.shape, 0)
     live_tile = jnp.zeros(live_send.shape, jnp.int32)
     for order in range(span_count):
-        live_tile = jnp.where(live_row == order, live_ref[flip_bits(near, order), 0], live_tile)
+        live_tile = jnp.where(live_row == order, live_ref[0, flip_bits(near, order)], live_tile)
     live_send[...] = live_tile
 
     pl.semaphore_wait(barrier, devices - 1)
@@ -319,7 +333,7 @@
         cache_copies[order, 1].wait_recv()
 
         column = lax.broadcasted_iota(jnp.int32, (1, slots), 1)
-        own_live = live_ref[flip_bits(near, order), 0]
+        own_live = live_ref[0, flip_bits(near, order)]
         peer_live = jnp.broadcast_to(live_recv[order : order + 1, 0:1], (1, slots))
         bias = jnp.concatenate(
             [
@@ -453,16 +467,22 @@
     rows = half_kv * group_size * share
     turns = jnp.concatenate([turn_table(HD)] * 2)[None, :]
     vmem = pl.BlockSpec(memory_space=pltpu.VMEM)
-    smem = pl.BlockSpec(memory_space=pltpu.SMEM)
-    hbm = pl.BlockSpec(memory_space=pl.ANY)
+    hbm = pl.BlockSpec(memory_space=pltpu.HBM)
     dma = pltpu.SemaphoreType.DMA
     bf16 = jnp.bfloat16
     return pl.pallas_call(
         functools.partial(attend_kernel, devices, spans, kv_heads, group_size),
         out_shape=jax.ShapeDtypeStruct(query_in.shape, bf16),
-        in_specs=[vmem, vmem, vmem, vmem, hbm, hbm, smem, smem],
+        in_specs=[hbm] * 8,
         out_specs=vmem,
         scratch_shapes=[
+            pltpu.VMEM(turns.shape, jnp.int32),
+            pltpu.VMEM(query_in.shape, bf16),
+            pltpu.VMEM(key_in.shape, bf16),
+            pltpu.VMEM(value_in.shape, bf16),
+            pltpu.SMEM((1, spans), jnp.int32),
+            pltpu.SMEM((spans,), jnp.int32),
+            dma((6,)),
             pltpu.VMEM((devices, rows, HD), bf16),
             pltpu.VMEM((rows, HD), bf16),
             pltpu.VMEM((spans, 2 * slots, half_kv * HD), bf16),
@@ -481,10 +501,10 @@
             dma((2,)), dma((2,)),
         ],
         compiler_params=pltpu.CompilerParams(
-            collective_id=0, has_side_effects=True, vmem_limit_bytes=40 * 2**20
+            collective_id=0, has_side_effects=True, vmem_limit_bytes=64 * 2**20 - 65536
         ),
         name="fused_attention",
-    )(turns, query_in, key_in, value_in, cache_keys, cache_values, live_slots, span_starts)
+    )(turns, query_in, key_in, value_in, cache_keys, cache_values, live_slots.T, span_starts)
 
 
 def is_power(number):

time: 31.4 us -> 26.8 us (0.85)
  local copies, waits for them, and re-layouts: 5.81 us -> 1.38 us
    unnamed x16 -> x1, local copies, waits for them, and re-layouts: 5.81 us -> 1.38 us
where the time goes in v2:
time: 26.8 us; the launch traced here: 26.6 us
  Pallas kernels  25.2 us (94%)
  local copies, waits for them, and re-layouts  1.38 us (5%)
    pallas_call x1, Pallas kernels, fused_device(): pl.pallas_call(functools.partial(attend_kernel, devices, spans, kv_heads,...  25.2 us
    unnamed x1, local copies, waits for them, and re-layouts  1.38 us

profile of v2, /device:TPU:0, one launch (start us, length us, event | category | flops | bytes accessed | tf_op | source)
XLA Modules:
  0.0 26.6 jit_solution(13339863602466837721)
XLA Ops:
  0.0 25.2 %fused_attention.1 = bf16[8,2048]{1,0:T(8,128)(2,1)} custom-call(s32[1,128]{1,0:T(1,128)} %constant.8.turn_hbm, bf16[8,2048]{1,0:T(8,128)(2,1)} %query_hbm.1, bf16[8,512]{1,0:T(8,128)(2,1)} %key_hbm.1, bf16[8,512]{1,0:T(8,128)(2,1)} %value_hbm.1, bf16[2,384,512]{2,1,0:T(8,128)(2,1)} %cache_k.1, bf16[2,384,512]{2,1,0:T(8,128)(2,1)} %cache_v.1, ...), custom_call_target="tpu_custom_call" | custom-call | tf_op jit(solution)/shard_map/fused_attention/pallas_call | solution.py:473
  25.2 1.4 %copy.10 = bf16[8,2048]{1,0:T(8,128)(2,1)} copy(bf16[8,2048]{1,0:T(8,128)(2,1)} %fused_attention.1) | data formatting | bytes 65536

commit v3 on v2

--- a/solution.py
+++ b/solution.py
@@ -295,12 +295,14 @@
     for mask in range(1, devices):
         src = q_slots.at[0] if mask % 2 == 0 else q_other
         q_copies[mask] = remote(src, q_slots.at[mask], q_ssem.at[mask], q_rsem.at[mask], mask)
-    for mask in range(devices - 1, span_devices - 1, -1):
-        q_copies[mask].start()
-    for mask in range(1, span_devices):
-        q_copies[mask].start()
+    split = span_devices // 2
+    early = [(order, order * span_devices, split) for order in range(1, span_count)]
+    late = [(order, begin + split, split) for order, begin, unused in early]
+    units = early + [(0, 0, span_devices)] + late
+
     cache_copies = {}
-    for order in range(span_count):
+
+    def swap_cache(order):
         span = flip_bits(near, order)
         for which, (src, dst) in enumerate(((cache_k, k_buf), (cache_v, v_buf))):
             copy = remote(
@@ -310,27 +312,38 @@
             )
             copy.start()
             cache_copies[order, which] = copy
-        if order == 0:
-            new_copy = remote(new_send, new_recv, misc_ssem.at[0], misc_rsem.at[0], 1)
-            new_copy.start()
-            live_copy = remote(live_send, live_recv, misc_ssem.at[1], misc_rsem.at[1], 1)
-            live_copy.start()
+
+    for unused, begin, count in early:
+        for mask in range(begin, begin + count):
+            q_copies[mask].start()
+    live_copy = remote(live_send, live_recv, misc_ssem.at[1], misc_rsem.at[1], 1)
+    live_copy.start()
+    for order in range(1, span_count):
+        swap_cache(order)
+    for unused, begin, count in late:
+        for mask in range(begin, begin + count):
+            q_copies[mask].start()
+    for mask in range(1, span_devices):
+        q_copies[mask].start()
+    new_copy = remote(new_send, new_recv, misc_ssem.at[0], misc_rsem.at[0], 1)
+    new_copy.start()
+    swap_cache(0)
 
     stat_lane = lax.broadcasted_iota(jnp.int32, (share, HD), 1)
     group_rows = group_size * share
-    o_copies = []
-
-    for order in range(span_count):
-        first_slot = order * span_devices
-        for mask in range(max(first_slot, 1), first_slot + span_devices):
+    o_copies = {mask: [] for mask in range(1, devices)}
+
+    live_copy.wait_recv()
+    for order, first_slot, count in units:
+        for mask in range(max(first_slot, 1), first_slot + count):
             q_copies[mask].wait_recv()
         if order == 0:
             new_copy.wait_recv()
-            live_copy.wait_recv()
-        local_copies[2 * order].wait()
-        local_copies[2 * order + 1].wait()
-        cache_copies[order, 0].wait_recv()
-        cache_copies[order, 1].wait_recv()
+        if first_slot == order * span_devices:
+            local_copies[2 * order].wait()
+            local_copies[2 * order + 1].wait()
+            cache_copies[order, 0].wait_recv()
+            cache_copies[order, 1].wait_recv()
 
         column = lax.broadcasted_iota(jnp.int32, (1, slots), 1)
         own_live = live_ref[0, flip_bits(near, order)]
@@ -342,7 +355,7 @@
             ],
             axis=1,
         )
-        row_total = span_devices * group_rows
+        row_total = count * group_rows
         if order == 0:
             filler = jnp.zeros((HD - 2 * share, half_lanes), jnp.float32)
             received = new_recv[...].astype(jnp.float32)
@@ -368,10 +381,10 @@
                 pieces.extend([piece] * group_size)
             new_bias = jnp.concatenate(pieces, axis=0)
 
-        stats = [jnp.zeros((share, HD), jnp.float32) for unused in range(span_devices)]
+        stats = [jnp.zeros((share, HD), jnp.float32) for unused in range(count)]
         for g in range(half_kv):
             queries = q_slots[
-                first_slot : first_slot + span_devices, g * group_rows : (g + 1) * group_rows, :
+                first_slot : first_slot + count, g * group_rows : (g + 1) * group_rows, :
             ].reshape(row_total, HD)
             head_lanes = slice(g * HD, (g + 1) * HD)
             nt = (((1,), (1,)), ((), ()))
@@ -399,9 +412,9 @@
                     preferred_element_type=jnp.float32,
                 )
             o_send[
-                first_slot : first_slot + span_devices, g * group_rows : (g + 1) * group_rows, :
-            ] = sums.astype(jnp.bfloat16).reshape(span_devices, group_rows, HD)
-            for member in range(span_devices):
+                first_slot : first_slot + count, g * group_rows : (g + 1) * group_rows, :
+            ] = sums.astype(jnp.bfloat16).reshape(count, group_rows, HD)
+            for member in range(count):
                 for h in range(group_size):
                     begin = member * group_rows + h * share
                     where = g * group_size + h
@@ -411,9 +424,9 @@
                     stats[member] = jnp.where(
                         stat_lane == where + HD // 2, totals[begin : begin + share], stats[member]
                     )
-        for member in range(span_devices):
+        for member in range(count):
             s_send[first_slot + member] = stats[member]
-        for member in reversed(range(span_devices)):
+        for member in range(count):
             mask = first_slot + member
             if mask == 0:
                 continue
@@ -423,35 +436,53 @@
             ):
                 copy = remote(src.at[mask], dst.at[mask], ssem.at[mask], rsem.at[mask], mask)
                 copy.start()
-                o_copies.append(copy)
-
-    for copy in o_copies:
-        copy.wait_recv()
+                o_copies[mask].append(copy)
+
+    late_masks = [m for unused, begin, count in late for m in range(begin, begin + count)]
+    early_masks = [m for m in range(devices) if m not in late_masks]
+    state = {}
+    for masks in (early_masks, late_masks):
+        for mask in masks:
+            for copy in o_copies.get(mask, []):
+                copy.wait_recv()
+        for parity in range(2):
+            members = [m for m in masks if m % 2 == parity]
+            stat = [s_send[0] if m == 0 else s_recv[m] for m in members]
+            top = functools.reduce(jnp.maximum, stat)
+            total = None
+            accumulated = [None] * half_heads
+            if parity in state:
+                old_top, old_total, old_accumulated = state[parity]
+                top = jnp.maximum(top, old_top)
+                factor = jnp.exp2((old_top - top) * scale2)
+                total = old_total * factor
+                accumulated = [
+                    factor[:, head : head + 1] * old_accumulated[head]
+                    for head in range(half_heads)
+                ]
+            for member, s in zip(members, stat):
+                factor = jnp.exp2((s - top) * scale2)
+                part = factor * pltpu.roll(s, HD // 2, 1)
+                total = part if total is None else total + part
+                block = (o_send[0] if member == 0 else o_recv[member]).astype(jnp.float32)
+                for head in range(half_heads):
+                    term = factor[:, head : head + 1] * block[head * share : (head + 1) * share]
+                    accumulated[head] = (
+                        term if accumulated[head] is None else accumulated[head] + term
+                    )
+            state[parity] = (top, total, accumulated)
 
     for parity in range(2):
-        masks = list(range(parity, devices, 2))
-        stat = [s_send[0] if mask == 0 else s_recv[mask] for mask in masks]
-        top = functools.reduce(jnp.maximum, stat)
-        factors = [jnp.exp2((s - top) * scale2) for s in stat]
-        total = functools.reduce(
-            jnp.add, [f * pltpu.roll(s, HD // 2, 1) for f, s in zip(factors, stat)]
-        )
+        unused_top, total, accumulated = state[parity]
         inverse = 1.0 / total
-        accumulated = [None] * half_heads
-        for f, mask in zip(factors, masks):
-            weight = f * inverse
-            block = (o_send[0] if mask == 0 else o_recv[mask]).astype(jnp.float32)
-            for head in range(half_heads):
-                term = weight[:, head : head + 1] * block[head * share : (head + 1) * share]
-                accumulated[head] = (
-                    term if accumulated[head] is None else accumulated[head] + term
-                )
         which = half if parity == 0 else 1 - half
         out_ref[:, lanes(which, half_heads * HD)] = jnp.concatenate(
-            accumulated, axis=1
+            [accumulated[head] * inverse[:, head : head + 1] for head in range(half_heads)],
+            axis=1,
         ).astype(jnp.bfloat16)
 
-    for copy in list(q_copies.values()) + list(cache_copies.values()) + o_copies:
+    result_copies = [copy for pair in o_copies.values() for copy in pair]
+    for copy in list(q_copies.values()) + list(cache_copies.values()) + result_copies:
         copy.wait_send()
     new_copy.wait_send()
     live_copy.wait_send()
@@ -518,7 +549,7 @@
     return (
         is_power(devices)
         and is_power(spans)
-        and devices >= 2 * spans
+        and devices >= 2 * spans and spans >= 2
         and query_in.shape[0] == 8
         and kv_heads % 2 == 0
         and query_in.shape[1] % key_in.shape[1] == 0

time: 26.8 us -> 25.6 us (0.955)
  Pallas kernels: 25.2 us -> 24 us
    pallas_call x1, Pallas kernels: 25.2 us -> 24 us  [fused_device(): pl.pallas_call(functools.partial(attend_kernel, devices, spans, kv_heads,...]
where the time goes in v3:
time: 25.6 us; the launch traced here: 25.4 us
  Pallas kernels  24 us (94%)
  local copies, waits for them, and re-layouts  1.38 us (5%)
    pallas_call x1, Pallas kernels, fused_device(): pl.pallas_call(functools.partial(attend_kernel, devices, spans, kv_heads,...  24 us
    unnamed x1, local copies, waits for them, and re-layouts  1.38 us

profile of v3, /device:TPU:0, one launch (start us, length us, event | category | flops | bytes accessed | tf_op | source)
XLA Modules:
  0.0 25.4 jit_solution(4374578706055868404)
XLA Ops:
  0.0 24.0 %fused_attention.1 = bf16[8,2048]{1,0:T(8,128)(2,1)} custom-call(s32[1,128]{1,0:T(1,128)} %constant.8.turn_hbm, bf16[8,2048]{1,0:T(8,128)(2,1)} %query_hbm.1, bf16[8,512]{1,0:T(8,128)(2,1)} %key_hbm.1, bf16[8,512]{1,0:T(8,128)(2,1)} %value_hbm.1, bf16[2,384,512]{2,1,0:T(8,128)(2,1)} %cache_k.1, bf16[2,384,512]{2,1,0:T(8,128)(2,1)} %cache_v.1, ...), custom_call_target="tpu_custom_call" | custom-call | tf_op jit(solution)/shard_map/fused_attention/pallas_call | solution.py:504
  24.0 1.4 %copy.10 = bf16[8,2048]{1,0:T(8,128)(2,1)} copy(bf16[8,2048]{1,0:T(8,128)(2,1)} %fused_attention.1) | data formatting | bytes 65536

commit v4 on v3

--- a/solution.py
+++ b/solution.py
@@ -176,6 +176,9 @@
     return lax.dynamic_slice_in_dim(attended, row_start, share_rows, 0)
 
 
+RELAY = 2
+
+
 def flip_bits(index, mask):
     result = index
     bit = 1
@@ -293,12 +296,19 @@
 
     q_copies = {}
     for mask in range(1, devices):
-        src = q_slots.at[0] if mask % 2 == 0 else q_other
-        q_copies[mask] = remote(src, q_slots.at[mask], q_ssem.at[mask], q_rsem.at[mask], mask)
+        sems = (q_ssem.at[mask], q_rsem.at[mask])
+        if mask & RELAY:
+            q_copies[mask] = remote(q_slots.at[mask - RELAY], q_slots.at[mask], *sems, RELAY)
+        else:
+            src = q_slots.at[0] if mask % 2 == 0 else q_other
+            q_copies[mask] = remote(src, q_slots.at[mask], *sems, mask)
     split = span_devices // 2
     early = [(order, order * span_devices, split) for order in range(1, span_count)]
     late = [(order, begin + split, split) for order, begin, unused in early]
     units = early + [(0, 0, span_devices)] + late
+
+    def direct(begin, count):
+        return [mask for mask in range(begin, begin + count) if not mask & RELAY]
 
     cache_copies = {}
 
@@ -314,17 +324,18 @@
             cache_copies[order, which] = copy
 
     for unused, begin, count in early:
-        for mask in range(begin, begin + count):
+        for mask in direct(begin, count):
             q_copies[mask].start()
     live_copy = remote(live_send, live_recv, misc_ssem.at[1], misc_rsem.at[1], 1)
     live_copy.start()
     for order in range(1, span_count):
         swap_cache(order)
     for unused, begin, count in late:
-        for mask in range(begin, begin + count):
+        for mask in direct(begin, count):
             q_copies[mask].start()
-    for mask in range(1, span_devices):
+    for mask in direct(1, span_devices - 1):
         q_copies[mask].start()
+    q_copies[RELAY].start()
     new_copy = remote(new_send, new_recv, misc_ssem.at[0], misc_rsem.at[0], 1)
     new_copy.start()
     swap_cache(0)
@@ -333,10 +344,16 @@
     group_rows = group_size * share
     o_copies = {mask: [] for mask in range(1, devices)}
 
+    for unused, begin, count in early + late + [(0, 1, span_devices - 1)]:
+        for mask in direct(begin, count):
+            q_copies[mask].wait_recv()
+            q_copies[mask + RELAY].start()
+
     live_copy.wait_recv()
     for order, first_slot, count in units:
-        for mask in range(max(first_slot, 1), first_slot + count):
-            q_copies[mask].wait_recv()
+        for mask in range(first_slot, first_slot + count):
+            if mask & RELAY:
+                q_copies[mask].wait_recv()
         if order == 0:
             new_copy.wait_recv()
         if first_slot == order * span_devices:
@@ -549,7 +566,7 @@
     return (
         is_power(devices)
         and is_power(spans)
-        and devices >= 2 * spans and spans >= 2
+        and devices >= 8 * spans and spans >= 2
         and query_in.shape[0] == 8
         and kv_heads % 2 == 0
         and query_in.shape[1] % key_in.shape[1] == 0

time: 25.6 us -> 24.7 us (0.965)
  Pallas kernels: 24 us -> 23.1 us
    pallas_call x1, Pallas kernels: 24 us -> 23.1 us  [fused_device(): pl.pallas_call(functools.partial(attend_kernel, devices, spans, kv_heads,...]
where the time goes in v4:
time: 24.7 us; the launch traced here: 24.5 us
  Pallas kernels  23.1 us (94%)
  local copies, waits for them, and re-layouts  1.38 us (6%)
    pallas_call x1, Pallas kernels, fused_device(): pl.pallas_call(functools.partial(attend_kernel, devices, spans, kv_heads,...  23.1 us
    unnamed x1, local copies, waits for them, and re-layouts  1.38 us

profile of v4, /device:TPU:0, one launch (start us, length us, event | category | flops | bytes accessed | tf_op | source)
XLA Modules:
  0.0 24.5 jit_solution(16930227536808838102)
XLA Ops:
  0.0 23.1 %fused_attention.1 = bf16[8,2048]{1,0:T(8,128)(2,1)} custom-call(s32[1,128]{1,0:T(1,128)} %constant.8.turn_hbm, bf16[8,2048]{1,0:T(8,128)(2,1)} %query_hbm.1, bf16[8,512]{1,0:T(8,128)(2,1)} %key_hbm.1, bf16[8,512]{1,0:T(8,128)(2,1)} %value_hbm.1, bf16[2,384,512]{2,1,0:T(8,128)(2,1)} %cache_k.1, bf16[2,384,512]{2,1,0:T(8,128)(2,1)} %cache_v.1, ...), custom_call_target="tpu_custom_call" | custom-call | tf_op jit(solution)/shard_map/fused_attention/pallas_call | solution.py:521
  23.1 1.4 %copy.10 = bf16[8,2048]{1,0:T(8,128)(2,1)} copy(bf16[8,2048]{1,0:T(8,128)(2,1)} %fused_attention.1) | data formatting | bytes 65536

commit v5 on v4

--- a/solution.py
+++ b/solution.py
@@ -305,7 +305,7 @@
     split = span_devices // 2
     early = [(order, order * span_devices, split) for order in range(1, span_count)]
     late = [(order, begin + split, split) for order, begin, unused in early]
-    units = early + [(0, 0, span_devices)] + late
+    units = early + late + [(0, 0, span_devices)]
 
     def direct(begin, count):
         return [mask for mask in range(begin, begin + count) if not mask & RELAY]

time: 24.7 us -> 24.9 us (level)
  no operation moved by 1% of the time
where the time goes in v5:
time: 24.9 us; the launch traced here: 24.7 us
  Pallas kernels  23.3 us (94%)
  local copies, waits for them, and re-layouts  1.38 us (6%)
    pallas_call x1, Pallas kernels, fused_device(): pl.pallas_call(functools.partial(attend_kernel, devices, spans, kv_heads,...  23.3 us
    unnamed x1, local copies, waits for them, and re-layouts  1.38 us

profile of v5, /device:TPU:0, one launch (start us, length us, event | category | flops | bytes accessed | tf_op | source)
XLA Modules:
  0.0 24.7 jit_solution(7543192463614422330)
XLA Ops:
  0.0 23.3 %fused_attention.1 = bf16[8,2048]{1,0:T(8,128)(2,1)} custom-call(s32[1,128]{1,0:T(1,128)} %constant.8.turn_hbm, bf16[8,2048]{1,0:T(8,128)(2,1)} %query_hbm.1, bf16[8,512]{1,0:T(8,128)(2,1)} %key_hbm.1, bf16[8,512]{1,0:T(8,128)(2,1)} %value_hbm.1, bf16[2,384,512]{2,1,0:T(8,128)(2,1)} %cache_k.1, bf16[2,384,512]{2,1,0:T(8,128)(2,1)} %cache_v.1, ...), custom_call_target="tpu_custom_call" | custom-call | tf_op jit(solution)/shard_map/fused_attention/pallas_call | solution.py:521
  23.3 1.4 %copy.10 = bf16[8,2048]{1,0:T(8,128)(2,1)} copy(bf16[8,2048]{1,0:T(8,128)(2,1)} %fused_attention.1) | data formatting | bytes 65536

commit v6 on v4

--- a/solution.py
+++ b/solution.py
@@ -431,6 +431,14 @@
             o_send[
                 first_slot : first_slot + count, g * group_rows : (g + 1) * group_rows, :
             ] = sums.astype(jnp.bfloat16).reshape(count, group_rows, HD)
+            for mask in range(max(first_slot, 1), first_slot + count):
+                rows = pl.ds(g * group_rows, group_rows)
+                copy = remote(
+                    o_send.at[mask, rows], o_recv.at[mask, rows],
+                    o_ssem.at[mask, g], o_rsem.at[mask, g], mask,
+                )
+                copy.start()
+                o_copies[mask].append(copy)
             for member in range(count):
                 for h in range(group_size):
                     begin = member * group_rows + h * share
@@ -447,13 +455,11 @@
             mask = first_slot + member
             if mask == 0:
                 continue
-            for src, dst, ssem, rsem in (
-                (s_send, s_recv, s_ssem, s_rsem),
-                (o_send, o_recv, o_ssem, o_rsem),
-            ):
-                copy = remote(src.at[mask], dst.at[mask], ssem.at[mask], rsem.at[mask], mask)
-                copy.start()
-                o_copies[mask].append(copy)
+            copy = remote(
+                s_send.at[mask], s_recv.at[mask], s_ssem.at[mask], s_rsem.at[mask], mask
+            )
+            copy.start()
+            o_copies[mask].append(copy)
 
     late_masks = [m for unused, begin, count in late for m in range(begin, begin + count)]
     early_masks = [m for m in range(devices) if m not in late_masks]
@@ -543,7 +549,7 @@
             pltpu.VMEM((devices, rows, HD), bf16),
             pltpu.VMEM((devices, share, HD), jnp.float32),
             pltpu.VMEM((devices, share, HD), jnp.float32),
-            dma((devices,)), dma((devices,)), dma((devices,)), dma((devices,)),
+            dma((devices,)), dma((devices,)), dma((devices, half_kv)), dma((devices, half_kv)),
             dma((devices,)), dma((devices,)),
             dma((spans, 2)), dma((spans, 2)), dma((spans, 2)),
             dma((2,)), dma((2,)),

time: 24.7 us -> 25.1 us (1.016)
  Pallas kernels: 23.1 us -> 23.6 us
    pallas_call x1, Pallas kernels: 23.1 us -> 23.6 us  [fused_device(): pl.pallas_call(functools.partial(attend_kernel, devices, spans, kv_heads,...]
where the time goes in v6:
time: 25.1 us; the launch traced here: 24.9 us
  Pallas kernels  23.6 us (94%)
  local copies, waits for them, and re-layouts  1.38 us (5%)
    pallas_call x1, Pallas kernels, fused_device(): pl.pallas_call(functools.partial(attend_kernel, devices, spans, kv_heads,...  23.6 us
    unnamed x1, local copies, waits for them, and re-layouts  1.38 us

profile of v6, /device:TPU:0, one launch (start us, length us, event | category | flops | bytes accessed | tf_op | source)
XLA Modules:
  0.0 24.9 jit_solution(3654239871297379371)
XLA Ops:
  0.0 23.6 %fused_attention.1 = bf16[8,2048]{1,0:T(8,128)(2,1)} custom-call(s32[1,128]{1,0:T(1,128)} %constant.8.turn_hbm, bf16[8,2048]{1,0:T(8,128)(2,1)} %query_hbm.1, bf16[8,512]{1,0:T(8,128)(2,1)} %key_hbm.1, bf16[8,512]{1,0:T(8,128)(2,1)} %value_hbm.1, bf16[2,384,512]{2,1,0:T(8,128)(2,1)} %cache_k.1, bf16[2,384,512]{2,1,0:T(8,128)(2,1)} %cache_v.1, ...), custom_call_target="tpu_custom_call" | custom-call | tf_op jit(solution)/shard_map/fused_attention/pallas_call | solution.py:527
  23.6 1.4 %copy.10 = bf16[8,2048]{1,0:T(8,128)(2,1)} copy(bf16[8,2048]{1,0:T(8,128)(2,1)} %fused_attention.1) | data formatting | bytes 65536

commit v7 on v4

--- a/solution.py
+++ b/solution.py
@@ -194,8 +194,8 @@
     turn_hbm, query_hbm, key_hbm, value_hbm, cache_k, cache_v, live_hbm, start_hbm, out_ref,
     turn_ref, query_ref, key_ref, value_ref, live_ref, start_ref, in_sem,
     q_slots, q_other, k_buf, v_buf, new_send, new_recv, live_send, live_recv,
-    o_send, o_recv, s_send, s_recv,
-    q_ssem, q_rsem, o_ssem, o_rsem, s_ssem, s_rsem, cache_ssem, cache_rsem, local_sem,
+    o_send, o_recv,
+    q_ssem, q_rsem, o_ssem, o_rsem, cache_ssem, cache_rsem, local_sem,
     misc_ssem, misc_rsem,
 ):
     share = query_hbm.shape[0]
@@ -203,6 +203,7 @@
     half_kv = kv_heads // 2
     half_heads = half_kv * group_size
     half_lanes = half_kv * HD
+    stat_begin = half_heads * share
     span_devices = devices // span_count
     span_len = share * span_devices
     scale2 = HD ** (-0.5) * math.log2(math.e)
@@ -442,13 +443,18 @@
                         stat_lane == where + HD // 2, totals[begin : begin + share], stats[member]
                     )
         for member in range(count):
-            s_send[first_slot + member] = stats[member]
+            value = stats[member]
+            high = value.astype(jnp.bfloat16).astype(jnp.float32)
+            middle = (value - high).astype(jnp.bfloat16).astype(jnp.float32)
+            low = pltpu.roll(value - high - middle, half_heads, 1)
+            o_send[first_slot + member, stat_begin : stat_begin + 2 * share, :] = (
+                jnp.concatenate([high, middle + low], axis=0).astype(jnp.bfloat16)
+            )
         for member in range(count):
             mask = first_slot + member
             if mask == 0:
                 continue
             for src, dst, ssem, rsem in (
-                (s_send, s_recv, s_ssem, s_rsem),
                 (o_send, o_recv, o_ssem, o_rsem),
             ):
                 copy = remote(src.at[mask], dst.at[mask], ssem.at[mask], rsem.at[mask], mask)
@@ -464,7 +470,13 @@
                 copy.wait_recv()
         for parity in range(2):
             members = [m for m in masks if m % 2 == parity]
-            stat = [s_send[0] if m == 0 else s_recv[m] for m in members]
+            stat = []
+            for m in members:
+                packed = (o_send if m == 0 else o_recv)[
+                    m, stat_begin : stat_begin + 2 * share, :
+                ].astype(jnp.float32)
+                rest = packed[share:]
+                stat.append(packed[:share] + (rest + pltpu.roll(rest, HD - half_heads, 1)))
             top = functools.reduce(jnp.maximum, stat)
             total = None
             accumulated = [None] * half_heads
@@ -539,12 +551,9 @@
             pltpu.VMEM((2 * share, half_kv * HD), bf16),
             pltpu.VMEM((8, HD), jnp.int32),
             pltpu.VMEM((8, HD), jnp.int32),
-            pltpu.VMEM((devices, rows, HD), bf16),
-            pltpu.VMEM((devices, rows, HD), bf16),
-            pltpu.VMEM((devices, share, HD), jnp.float32),
-            pltpu.VMEM((devices, share, HD), jnp.float32),
+            pltpu.VMEM((devices, rows + 2 * share, HD), bf16),
+            pltpu.VMEM((devices, rows + 2 * share, HD), bf16),
             dma((devices,)), dma((devices,)), dma((devices,)), dma((devices,)),
-            dma((devices,)), dma((devices,)),
             dma((spans, 2)), dma((spans, 2)), dma((spans, 2)),
             dma((2,)), dma((2,)),
         ],
@@ -572,7 +581,7 @@
         and query_in.shape[1] % key_in.shape[1] == 0
         and cache_keys.shape[1] % 128 == 0
         and spans <= 8
-        and kv_heads // 2 * (query_in.shape[1] // key_in.shape[1]) <= 64
+        and kv_heads // 2 * (query_in.shape[1] // key_in.shape[1]) <= 16
     )
 
 

time: 24.7 us -> 24.4 us (0.988)
  Pallas kernels: 23.1 us -> 22.8 us
    pallas_call x1, Pallas kernels: 23.1 us -> 22.8 us  [fused_device(): pl.pallas_call(functools.partial(attend_kernel, devices, spans, kv_heads,...]
where the time goes in v7:
time: 24.4 us; the launch traced here: 24.2 us
  Pallas kernels  22.8 us (93%)
  local copies, waits for them, and re-layouts  1.38 us (6%)
    pallas_call x1, Pallas kernels, fused_device(): pl.pallas_call(functools.partial(attend_kernel, devices, spans, kv_heads,...  22.8 us
    unnamed x1, local copies, waits for them, and re-layouts  1.38 us

profile of v7, /device:TPU:0, one launch (start us, length us, event | category | flops | bytes accessed | tf_op | source)
XLA Modules:
  0.0 24.2 jit_solution(13127334986065692892)
XLA Ops:
  0.0 22.8 %fused_attention.1 = bf16[8,2048]{1,0:T(8,128)(2,1)} custom-call(s32[1,128]{1,0:T(1,128)} %constant.8.turn_hbm, bf16[8,2048]{1,0:T(8,128)(2,1)} %query_hbm.1, bf16[8,512]{1,0:T(8,128)(2,1)} %key_hbm.1, bf16[8,512]{1,0:T(8,128)(2,1)} %value_hbm.1, bf16[2,384,512]{2,1,0:T(8,128)(2,1)} %cache_k.1, bf16[2,384,512]{2,1,0:T(8,128)(2,1)} %cache_v.1, ...), custom_call_target="tpu_custom_call" | custom-call | tf_op jit(solution)/shard_map/fused_attention/pallas_call | solution.py:533
  22.9 1.4 %copy.10 = bf16[8,2048]{1,0:T(8,128)(2,1)} copy(bf16[8,2048]{1,0:T(8,128)(2,1)} %fused_attention.1) | data formatting | bytes 65536
